TPU v7x, 32 devices: a whole 2x2x4 slice. The times are simulated.
32 devices in a mesh: row: 4 (over y, core), col: 8 (over z, x).
Axes of the slice: x: 2, y: 2, z: 4, core: 2. Of those that a mesh axis runs over, the one named last changes fastest.
Arguments:
- features: bfloat16 [4096, 128], P(('row', 'col')), may hold values from -6 to 6
- norm_weight: float32 [4096], P(('row', 'col')), may hold values from 0.01767767 to 0.110485435
- weight_in: bfloat16 [128, 256], replicated, may hold values from -6 to 6
- weight_out: bfloat16 [256, 128], replicated, may hold values from -6 to 6
- labels: int32 [4096], P(('row', 'col')), may hold values from 0 to 127
- tile_slot: int32 [32, 128], P(('row', 'col')), may hold values from 0 to 31
- tile_edges: int32 [32, 128, 2, 512], P(('row', 'col')), may hold values from 0 to 127
- tile_count: int32 [32], P(('row', 'col')), may hold values from 32 to 128, as said below
Outputs:
- grad_in: float32 [128, 256], replicated
- grad_out: float32 [256, 128], replicated
- loss: float32 [], replicated
Inputs may be any that keep to these rules, and one draw needn't show every extreme that they name: `tile_slot`: position p of a slot covers the tile whose target rows start at 128 * (p // 4) and whose source columns start at 128 * (p % 4) within the device's block; a position may occur in several slots. Entry k of a slot marks row tile_edges[s, 0, k] and column tile_edges[s, 1, k] of its slot's tile; repeated entries count again. `tile_count`: slots at and after this number are not live; in every draw some device has all 128 slots live and another device only 32.
All inputs are finite; a program needn't handle non-finite values.
Results may differ from a plain program's by a relative error of at most 0.0084.
Values may be sent and summed in bfloat16 or wider, within the bound.
A program may use at most 64 MiB of HBM per device.

v0:
```python
import jax
import jax.numpy as jnp
from jax import lax
from jax.sharding import PartitionSpec as P

TILE = 128
SOFTCAP = 15.0
LOSS_SCALE = 1024.0
HIGHEST = lax.Precision.HIGHEST
CONTRACT_ROWS = (((0,), (0,)), ((), ()))


def densify(tile_slot, tile_edges, tile_count, row_group, col_group):
    tile_side = TILE
    col_tiles = col_group // tile_side
    row_tiles = row_group // tile_side
    slot_total = tile_slot.shape[0]
    offsets = jnp.arange(tile_side, dtype=jnp.int32)
    row_onehot = (tile_edges[:, 0, :, None] == offsets[None, None, :]).astype(jnp.bfloat16)
    col_onehot = (tile_edges[:, 1, :, None] == offsets[None, None, :]).astype(jnp.bfloat16)
    slot_tiles = jnp.einsum(
        "ser,sec->src", row_onehot, col_onehot, preferred_element_type=jnp.float32
    )
    slot_tiles = slot_tiles.astype(jnp.bfloat16).reshape(slot_total, tile_side * tile_side)
    slot_live = jnp.arange(slot_total, dtype=jnp.int32) < tile_count
    places = jnp.arange(row_tiles * col_tiles, dtype=jnp.int32)
    place_onehot = ((tile_slot[:, None] == places[None, :]) & slot_live[:, None]).astype(
        jnp.bfloat16
    )
    placed = lax.dot_general(
        place_onehot, slot_tiles, CONTRACT_ROWS, preferred_element_type=jnp.float32
    )
    placed = placed.astype(jnp.bfloat16).reshape(row_tiles, col_tiles, tile_side, tile_side)
    return placed.transpose(0, 2, 1, 3).reshape(row_group, col_group)


def gather_targets(values):
    return lax.all_gather(values, "col", axis=0, tiled=True)


def sum_sources(partial_sums):
    return lax.psum_scatter(partial_sums, "row", scatter_dimension=0, tiled=True)


def per_device(
    features, norm_weight, weight_in, weight_out, labels, tile_slot, tile_edges, tile_count
):
    row_size = lax.axis_size("row")
    col_size = lax.axis_size("col")
    node_rows = features.shape[0]
    total_nodes = node_rows * row_size * col_size
    adjacency = densify(
        tile_slot[0], tile_edges[0], tile_count[0], node_rows * col_size, node_rows * row_size
    )
    node_scale = norm_weight[:, None]
    normed = (node_scale * features.astype(jnp.float32)).astype(jnp.bfloat16)
    source_one = jnp.dot(normed, weight_in, preferred_element_type=jnp.float32)
    gathered_one = lax.all_gather(source_one, "row", axis=0, tiled=True)
    forward_one = jnp.dot(adjacency.astype(jnp.float32), gathered_one, precision=HIGHEST)
    projected = lax.psum_scatter(forward_one, "col", scatter_dimension=0, tiled=True)
    pre_hidden = node_scale * (projected + source_one)
    hidden = jax.nn.relu(pre_hidden).astype(jnp.bfloat16)
    source_two = (
        node_scale * jnp.dot(hidden, weight_out, preferred_element_type=jnp.float32)
    ).astype(jnp.bfloat16)
    gathered_two = lax.all_gather(source_two, "row", axis=0, tiled=True)
    forward_two = jnp.dot(adjacency, gathered_two, preferred_element_type=jnp.float32)
    logits = node_scale * (
        lax.psum_scatter(forward_two, "col", scatter_dimension=0, tiled=True)
        + source_two.astype(jnp.float32)
    )
    capped = SOFTCAP * jnp.tanh(logits / SOFTCAP)
    exp_capped = jnp.exp(capped)
    exp_total = jnp.sum(exp_capped, axis=1, keepdims=True)
    one_hot = (labels[:, None] == jnp.arange(capped.shape[1], dtype=jnp.int32)[None, :]).astype(
        jnp.float32
    )
    loss_local = jnp.sum(jnp.log(exp_total[:, 0]) - jnp.sum(capped * one_hot, axis=1))
    d_logits = (
        LOSS_SCALE
        / total_nodes
        * (exp_capped / exp_total - one_hot)
        * (1.0 - (capped / SOFTCAP) ** 2)
    )
    back_two = (node_scale * d_logits).astype(jnp.bfloat16)
    backward_two = lax.dot_general(
        adjacency, gather_targets(back_two), CONTRACT_ROWS, preferred_element_type=jnp.float32
    )
    d_source_two = node_scale * (sum_sources(backward_two) + back_two.astype(jnp.float32))
    grad_out_local = lax.dot_general(
        hidden.astype(jnp.float32), d_source_two, CONTRACT_ROWS, precision=HIGHEST
    )
    d_hidden = lax.dot_general(
        d_source_two, weight_out.astype(jnp.float32), (((1,), (1,)), ((), ())), precision=HIGHEST
    )
    back_one = (node_scale * jnp.where(pre_hidden > 0, d_hidden, 0.0)).astype(jnp.bfloat16)
    gathered_back = gather_targets(back_one)
    backward_one = lax.dot_general(
        adjacency, gathered_back, CONTRACT_ROWS, preferred_element_type=jnp.float32
    )
    d_source_one = sum_sources(backward_one) + back_one.astype(jnp.float32)
    grad_in_local = lax.dot_general(
        normed.astype(jnp.float32), d_source_one, CONTRACT_ROWS, precision=HIGHEST
    )
    grad_in, grad_out, loss_sum = lax.psum(
        (grad_in_local, grad_out_local, loss_local), ("row", "col")
    )
    return (grad_in, grad_out, loss_sum / total_nodes)


def solution(mesh):
    in_specs = (
        P(("row", "col"), None),
        P(("row", "col")),
        P(),
        P(),
        P(("row", "col")),
        P(("row", "col"), None),
        P(("row", "col"), None, None, None),
        P(("row", "col")),
    )
    out_specs = (P(), P(), P())
    return jax.shard_map(
        per_device, mesh=mesh, in_specs=in_specs, out_specs=out_specs, check_vma=False
    )
```

profile of v0, /device:TPU:0, one launch (start us, length us, event | category | flops | bytes accessed | tf_op | source)
XLA Modules:
  0.0 426.0 jit_solution(7901533714446784060)
XLA Ops:
  7.2 0.0 copy-start
  7.2 0.0 reduce-scatter.5.cloned.1.call-start
  7.2 1.7 fusion.37
  9.0 7.9 %iota_compare_fusion.17 = pred[128,512,128]{1,2,0:T(32,128)(4,1)} fusion(s32[128,512]{1,0:T(8,128)S(1)} %get-tuple-element.10), kind=kLoop, calls=%fused_computation.1.clone.clone.clone.clone.2 | loop fusion | flops 8388608 | bytes 8650752 | tf_op jit(solution)/shard_map/ser,sec->src/dot_general | solution.py:21
  17.6 0.0 copy-start.6
  17.6 14.4 %fusion.5 = bf16[128,128,128]{2,1,0:T(8,128)(2,1)S(1)} fusion(s32[128,512]{1,0:T(8,128)S(1)} %get-tuple-element.9, pred[128,512,128]{1,2,0:T(32,128)(4,1)} %iota_compare_fusion.17), kind=kOutput, calls=%fused_computation.8 | convolution fusion | flops 2157969408 | bytes 12845056 | tf_op jit(solution)/shard_map/ser,sec->src/dot_general | solution.py:21
  32.0 0.0 copy-start.4
  32.0 0.0 copy-start.2
  32.0 0.0 copy-start.3
  32.1 0.0 copy-done.6
  32.1 0.0 copy-start.5
  32.1 2.6 fusion.6
  34.7 0.2 copy.23
  34.9 0.7 copy.15
  35.7 0.1 copy.14
  35.8 0.2 fusion.34
  36.0 8.6 %all_gather.12 = f32[512,256]{1,0:T(8,128)S(1)} all-gather(f32[128,256]{1,0:T(8,128)S(1)} %fusion.34), channel_id=1, replica_groups=mesh['row'=4,'col'=8] {'row'}, dimensions={0}, use_global_device_ids=true | all-gather | bytes 655360 | tf_op jit(solution)/shard_map/all_gather | solution.py:58
  44.6 2.2 fusion.18
  46.8 0.0 reduce-scatter.5.cloned.1.call-update
  46.9 0.0 reduce-scatter.7.cloned.1.call-start
  46.9 64.4 %reduce-scatter.5.cloned.1.call-done = f32[128,256]{1,0:T(8,128)} async-done(((f32[1024,256]{1,0:T(8,128)}), f32[128,256]{1,0:T(8,128)}) %reduce-scatter.5.cloned.1.call-update) | async-done | bytes 131088 | tf_op jit(solution)/shard_map/reduce_scatter | solution.py:60
  111.3 1.2 fusion.11
  112.6 5.4 %all_gather.13 = bf16[512,128]{0,1:T(8,128)(2,1)S(1)} all-gather(bf16[128,128]{0,1:T(8,128)(2,1)S(1)} %fusion.11), channel_id=1, replica_groups=mesh['row'=4,'col'=8] {'row'}, dimensions={0}, use_global_device_ids=true | all-gather | bytes 163840 | tf_op jit(solution)/shard_map/all_gather | solution.py:66
  118.0 1.1 fusion.16
  119.1 0.0 reduce-scatter.7.cloned.1.call-update
  119.1 0.0 reduce-scatter.9.cloned.1.call-start
  119.2 61.5 %reduce-scatter.7.cloned.1.call-done = f32[128,128]{0,1:T(8,128)} async-done(((f32[1024,128]{0,1:T(8,128)}), f32[128,128]{0,1:T(8,128)}) %reduce-scatter.7.cloned.1.call-update) | async-done | bytes 65552 | tf_op jit(solution)/shard_map/reduce_scatter | solution.py:69
  180.7 0.9 select_reduce_fusion
  181.6 0.9 multiply_convert_fusion
  182.5 26.7 %all_gather.14 = bf16[1024,128]{0,1:T(8,128)(2,1)S(1)} all-gather(bf16[128,128]{0,1:T(8,128)(2,1)S(1)} %multiply_convert_fusion), channel_id=1, replica_groups=mesh['row'=4,'col'=8] {'col'}, dimensions={0}, use_global_device_ids=true | all-gather | bytes 294912 | tf_op jit(solution)/shard_map/all_gather | solution.py:38
  209.2 1.2 fusion.14
  210.3 0.0 reduce-scatter.9.cloned.1.call-update
  210.4 0.0 reduce-scatter.11.cloned.1.call-start
  210.4 17.7 %reduce-scatter.9.cloned.1.call-done = f32[128,128]{0,1:T(8,128)} async-done(((f32[512,128]{0,1:T(8,128)}), f32[128,128]{0,1:T(8,128)}) %reduce-scatter.9.cloned.1.call-update) | async-done | bytes 65552 | tf_op jit(solution)/shard_map/reduce_scatter | solution.py:42
  228.1 1.2 fusion.10
  229.3 31.4 %all_gather.15 = bf16[1024,256]{1,0:T(8,128)(2,1)S(1)} all-gather(bf16[128,256]{1,0:T(8,128)(2,1)S(1)} %fusion.10), channel_id=1, replica_groups=mesh['row'=4,'col'=8] {'col'}, dimensions={0}, use_global_device_ids=true | all-gather | bytes 589824 | tf_op jit(solution)/shard_map/all_gather | solution.py:38
  260.7 1.2 fusion.12
  262.0 0.0 reduce-scatter.11.cloned.1.call-update
  262.0 0.0 all-reduce.3.cloned.1.call-start
  262.0 1.8 fusion.29
  263.9 20.0 %reduce-scatter.11.cloned.1.call-done = f32[128,256]{1,0:T(8,128)} async-done(((f32[512,256]{1,0:T(8,128)}), f32[128,256]{1,0:T(8,128)}) %reduce-scatter.11.cloned.1.call-update) | async-done | bytes 131088 | tf_op jit(solution)/shard_map/reduce_scatter | solution.py:42
  283.8 1.8 fusion.24
  285.6 0.0 all-reduce.3.cloned.1.call-update
  285.7 0.6 subtract_reduce_fusion
  286.3 39.5 %psum.23 = f32[]{:T(128)} all-reduce(f32[]{:T(128)} %subtract_reduce_fusion), channel_id=1, replica_groups=mesh['row'=4,'col'=8] {'row','col'}, use_global_device_ids=true, to_apply=%region_9.10 | all-reduce | flops 1 | bytes 8 | tf_op jit(solution)/shard_map/psum | solution.py:105
  326.5 88.7 %all-reduce.3.cloned.1.call-done = (f32[128,256]{1,0:T(8,128)}, f32[256,128]{1,0:T(8,128)}) async-done(((f32[128,256]{1,0:T(8,128)}, f32[256,128]{1,0:T(8,128)}), (f32[128,256]{1,0:T(8,128)}, f32[256,128]{1,0:T(8,128)})) %all-reduce.3.cloned.1.call-update) | async-done | bytes 262160 | tf_op jit(solution)/shard_map/psum | solution.py:105
  415.2 1.6 copy.54
  416.7 1.6 copy.55
  (9 shorter events, 0.1 us)
Async XLA Ops:
  7.2 104.2 %copy-start = (bf16[256,128]{1,0:T(8,128)(2,1)S(1)}, bf16[256,128]{1,0:T(8,128)(2,1)}, u32[]{:S(2)}) copy-start(bf16[256,128]{1,0:T(8,128)(2,1)} %param.11) | copy-start | bytes 196612
  7.2 104.1 %reduce-scatter.5.cloned.1.call-start = ((), (), s32[]{:S(2)}) async-start(), calls=%async_computation.4 | async-start | bytes 1179648 | tf_op jit(solution)/shard_map/reduce_scatter | solution.py:60
  17.6 14.5 %copy-start.6 = (s32[1,128]{1,0:T(1,128)S(1)}, s32[1,128]{1,0:T(1,128)}, u32[]{:S(2)}) copy-start(s32[1,128]{1,0:T(1,128)} %param.13) | copy-start | bytes 1540
  32.0 3.6 copy-start.4
  32.0 3.7 copy-start.2
  32.0 3.7 copy-start.3
  32.1 148.6 %copy-start.5 = (s32[128]{0:T(128)S(1)}, s32[128]{0:T(128)}, u32[]{:S(2)}) copy-start(s32[128]{0:T(128)} %param.12) | copy-start | bytes 1540
  46.9 133.8 %reduce-scatter.7.cloned.1.call-start = ((), (), s32[]{:S(2)}) async-start(), calls=%async_computation.5 | async-start | bytes 589824 | tf_op jit(solution)/shard_map/reduce_scatter | solution.py:69
  111.3 150.7 %copy-start.1 = (f32[128,256]{1,0:T(8,128)S(1)}, f32[128,256]{1,0:T(8,128)}, u32[]{:S(2)}) copy-start(f32[128,256]{1,0:T(8,128)} %reduce-scatter.5.cloned.1.call-done) | copy-start | bytes 393220
  119.1 109.0 %reduce-scatter.9.cloned.1.call-start = ((), (), s32[]{:S(2)}) async-start(), calls=%async_computation.6 | async-start | bytes 327680 | tf_op jit(solution)/shard_map/reduce_scatter | solution.py:42
  210.4 73.5 %reduce-scatter.11.cloned.1.call-start = ((), (), s32[]{:S(2)}) async-start(), calls=%async_computation.7 | async-start | bytes 655360 | tf_op jit(solution)/shard_map/reduce_scatter | solution.py:42
  262.0 153.2 %all-reduce.3.cloned.1.call-start = ((), (), s32[]{:S(2)}) async-start(), calls=%async_computation.8 | async-start | bytes 524288 | tf_op jit(solution)/shard_map/psum | solution.py:105
Sparse Core Ops, SparseCore 0:
  47.0 64.3 reduce-scatter.4
  119.2 61.4 reduce-scatter.6
  210.5 17.5 reduce-scatter.8
  262.1 21.6 reduce-scatter.10
  289.9 125.1 all-reduce.2
where the time goes:
time: 426 us
  waiting for transfers between devices  252 us (59%)
  blocking collectives  112 us (26%)
  matrix products  29 us (7%)
  between operations  16.4 us (4%)
  other arithmetic  10.3 us (2%)
  local copies, waits for them, and re-layouts  6.02 us (1%)
    psum x1, waiting for transfers between devices, per_device(): lax.psum((grad_in_local, grad_out_local, loss_local), ('row', 'col'))  88.7 us
    reduce_scatter x1, waiting for transfers between devices, per_device(): lax.psum_scatter(forward_one, 'col', scatter_dimension=0, tiled=True)  64.4 us
    reduce_scatter x1, waiting for transfers between devices, per_device(): lax.psum_scatter(forward_two, 'col', scatter_dimension=0, tiled=True)  61.5 us
    all_gather x2, blocking collectives, gather_targets(): return lax.all_gather(values, 'col', axis=0, tiled=True)  58.1 us
    psum x1, blocking collectives, per_device(): lax.psum((grad_in_local, grad_out_local, loss_local), ('row', 'col'))  39.5 us
    reduce_scatter x2, waiting for transfers between devices, sum_sources(): lax.psum_scatter(partial_sums, 'row', scatter_dimension=0, tiled=True)  37.7 us
    dot_general x1, matrix products, densify(): jnp.einsum('ser,sec->src', row_onehot, col_onehot, preferred_element_type...  14.4 us
    all_gather x1, blocking collectives, per_device(): gathered_one = lax.all_gather(source_one, 'row', axis=0, tiled=True)  8.65 us
  transfers between devices with their start and end apart: 5, of which 5 were waited for; matrix products, arithmetic and copies ran while one was open for 1% of the time, Pallas kernels for 0%

commit v1 on v0

--- a/solution.py
+++ b/solution.py
@@ -8,6 +8,11 @@
 LOSS_SCALE = 1024.0
 HIGHEST = lax.Precision.HIGHEST
 CONTRACT_ROWS = (((0,), (0,)), ((), ()))
+
+
+def cover_face(inputs):
+    arr_out = jax.lax.psum(inputs, "col")
+    return jax.lax.psum(arr_out, axis_name="row")
 
 
 def densify(tile_slot, tile_edges, tile_count, row_group, col_group):
@@ -102,9 +107,7 @@
     grad_in_local = lax.dot_general(
         normed.astype(jnp.float32), d_source_one, CONTRACT_ROWS, precision=HIGHEST
     )
-    grad_in, grad_out, loss_sum = lax.psum(
-        (grad_in_local, grad_out_local, loss_local), ("row", "col")
-    )
+    grad_in, grad_out, loss_sum = cover_face((grad_in_local, grad_out_local, loss_local))
     return (grad_in, grad_out, loss_sum / total_nodes)
 
 

time: 426 us -> 404 us (0.948)
  blocking collectives: 112 us -> 98.6 us
  waiting for transfers between devices: 252 us -> 243 us
    psum x1 -> x2, blocking collectives: 39.5 us -> 26.6 us  [the longest x1 20.4 us: cover_face(): arr_out = jax.lax.psum(inputs, 'col')]
    psum x1 -> x2, waiting for transfers between devices: 88.7 us -> 78.8 us  [the longest x1 72.9 us: cover_face(): arr_out = jax.lax.psum(inputs, 'col')]
  transfers between devices with their start and end apart: 5 -> 6, of which waited for: 5 -> 6; matrix products, arithmetic and copies ran while one was open for 1% -> 1% of each run, Pallas kernels for 0% -> 0%
where the time goes in v1:
time: 404 us
  waiting for transfers between devices  243 us (60%)
  blocking collectives  98.6 us (24%)
  matrix products  29 us (7%)
  between operations  16.7 us (4%)
  other arithmetic  10.3 us (3%)
  local copies, waits for them, and re-layouts  6.02 us (1%)
    psum x1, waiting for transfers between devices, cover_face(): arr_out = jax.lax.psum(inputs, 'col')  72.9 us
    reduce_scatter x1, waiting for transfers between devices, per_device(): lax.psum_scatter(forward_one, 'col', scatter_dimension=0, tiled=True)  64.7 us
    reduce_scatter x1, waiting for transfers between devices, per_device(): lax.psum_scatter(forward_two, 'col', scatter_dimension=0, tiled=True)  61.6 us
    all_gather x2, blocking collectives, gather_targets(): return lax.all_gather(values, 'col', axis=0, tiled=True)  57.9 us
    reduce_scatter x2, waiting for transfers between devices, sum_sources(): lax.psum_scatter(partial_sums, 'row', scatter_dimension=0, tiled=True)  37.7 us
    psum x1, blocking collectives, cover_face(): arr_out = jax.lax.psum(inputs, 'col')  20.4 us
    dot_general x1, matrix products, densify(): jnp.einsum('ser,sec->src', row_onehot, col_onehot, preferred_element_type...  14.4 us
    all_gather x1, blocking collectives, per_device(): gathered_one = lax.all_gather(source_one, 'row', axis=0, tiled=True)  8.65 us
  transfers between devices with their start and end apart: 6, of which 6 were waited for; matrix products, arithmetic and copies ran while one was open for 1% of the time, Pallas kernels for 0%

profile of v1, /device:TPU:0, one launch (start us, length us, event | category | flops | bytes accessed | tf_op | source)
XLA Modules:
  0.0 403.6 jit_solution(15084742050495321334)
XLA Ops:
  7.2 0.0 copy-start
  7.2 0.0 reduce-scatter.5.cloned.1.call-start
  7.2 1.7 fusion.37
  9.0 7.9 %iota_compare_fusion.17 = pred[128,512,128]{1,2,0:T(32,128)(4,1)} fusion(s32[128,512]{1,0:T(8,128)S(1)} %get-tuple-element.12), kind=kLoop, calls=%fused_computation.1.clone.clone.clone.clone.2 | loop fusion | flops 8388608 | bytes 8650752 | tf_op jit(solution)/shard_map/ser,sec->src/dot_general | solution.py:26
  17.6 14.4 %fusion.5 = bf16[128,128,128]{2,1,0:T(8,128)(2,1)S(1)} fusion(s32[128,512]{1,0:T(8,128)S(1)} %get-tuple-element.11, pred[128,512,128]{1,2,0:T(32,128)(4,1)} %iota_compare_fusion.17), kind=kOutput, calls=%fused_computation.8 | convolution fusion | flops 2157969408 | bytes 12845056 | tf_op jit(solution)/shard_map/ser,sec->src/dot_general | solution.py:26
  32.0 0.0 copy-start.4
  32.1 0.0 copy-start.5
  32.1 2.6 fusion.6
  34.7 0.2 copy.23
  34.9 0.7 copy.15
  35.7 0.1 copy.14
  35.8 0.2 fusion.34
  36.0 8.6 %all_gather.12 = f32[512,256]{1,0:T(8,128)S(1)} all-gather(f32[128,256]{1,0:T(8,128)S(1)} %fusion.34), channel_id=1, replica_groups=mesh['row'=4,'col'=8] {'row'}, dimensions={0}, use_global_device_ids=true | all-gather | bytes 655360 | tf_op jit(solution)/shard_map/all_gather | solution.py:63
  44.6 2.2 fusion.18
  46.8 0.0 reduce-scatter.5.cloned.1.call-update
  46.9 0.0 reduce-scatter.7.cloned.1.call-start
  46.9 64.7 %reduce-scatter.5.cloned.1.call-done = f32[128,256]{1,0:T(8,128)} async-done(((f32[1024,256]{1,0:T(8,128)}), f32[128,256]{1,0:T(8,128)}) %reduce-scatter.5.cloned.1.call-update) | async-done | bytes 131088 | tf_op jit(solution)/shard_map/reduce_scatter | solution.py:65
  111.6 1.2 fusion.11
  112.8 5.4 %all_gather.13 = bf16[512,128]{0,1:T(8,128)(2,1)S(1)} all-gather(bf16[128,128]{0,1:T(8,128)(2,1)S(1)} %fusion.11), channel_id=1, replica_groups=mesh['row'=4,'col'=8] {'row'}, dimensions={0}, use_global_device_ids=true | all-gather | bytes 163840 | tf_op jit(solution)/shard_map/all_gather | solution.py:71
  118.3 1.1 fusion.16
  119.4 0.0 reduce-scatter.7.cloned.1.call-update
  119.4 0.0 reduce-scatter.9.cloned.1.call-start
  119.5 61.6 %reduce-scatter.7.cloned.1.call-done = f32[128,128]{0,1:T(8,128)} async-done(((f32[1024,128]{0,1:T(8,128)}), f32[128,128]{0,1:T(8,128)}) %reduce-scatter.7.cloned.1.call-update) | async-done | bytes 65552 | tf_op jit(solution)/shard_map/reduce_scatter | solution.py:74
  181.0 0.9 select_reduce_fusion
  181.9 0.9 multiply_convert_fusion
  182.8 26.5 %all_gather.14 = bf16[1024,128]{0,1:T(8,128)(2,1)S(1)} all-gather(bf16[128,128]{0,1:T(8,128)(2,1)S(1)} %multiply_convert_fusion), channel_id=1, replica_groups=mesh['row'=4,'col'=8] {'col'}, dimensions={0}, use_global_device_ids=true | all-gather | bytes 294912 | tf_op jit(solution)/shard_map/all_gather | solution.py:43
  209.3 1.2 fusion.14
  210.5 0.0 reduce-scatter.9.cloned.1.call-update
  210.5 0.0 reduce-scatter.11.cloned.1.call-start
  210.6 17.7 %reduce-scatter.9.cloned.1.call-done = f32[128,128]{0,1:T(8,128)} async-done(((f32[512,128]{0,1:T(8,128)}), f32[128,128]{0,1:T(8,128)}) %reduce-scatter.9.cloned.1.call-update) | async-done | bytes 65552 | tf_op jit(solution)/shard_map/reduce_scatter | solution.py:47
  228.3 1.2 fusion.10
  229.5 31.4 %all_gather.15 = bf16[1024,256]{1,0:T(8,128)(2,1)S(1)} all-gather(bf16[128,256]{1,0:T(8,128)(2,1)S(1)} %fusion.10), channel_id=1, replica_groups=mesh['row'=4,'col'=8] {'col'}, dimensions={0}, use_global_device_ids=true | all-gather | bytes 589824 | tf_op jit(solution)/shard_map/all_gather | solution.py:43
  260.9 1.2 fusion.12
  262.1 0.0 reduce-scatter.11.cloned.1.call-update
  262.1 0.0 all-reduce.5.cloned.1.call-start
  262.2 1.8 fusion.29
  264.0 20.0 %reduce-scatter.11.cloned.1.call-done = f32[128,256]{1,0:T(8,128)} async-done(((f32[512,256]{1,0:T(8,128)}), f32[128,256]{1,0:T(8,128)}) %reduce-scatter.11.cloned.1.call-update) | async-done | bytes 131088 | tf_op jit(solution)/shard_map/reduce_scatter | solution.py:47
  284.0 1.8 fusion.24
  285.8 0.0 all-reduce.5.cloned.1.call-update
  285.8 0.0 all-reduce.7.cloned.1.call-start
  285.8 72.9 %all-reduce.5.cloned.1.call-done = (f32[128,256]{1,0:T(8,128)}, f32[256,128]{1,0:T(8,128)}) async-done(((f32[128,256]{1,0:T(8,128)}, f32[256,128]{1,0:T(8,128)}), (f32[128,256]{1,0:T(8,128)}, f32[256,128]{1,0:T(8,128)})) %all-reduce.5.cloned.1.call-update) | async-done | bytes 262160 | tf_op jit(solution)/shard_map/psum | solution.py:14
  358.7 0.0 all-reduce.7.cloned.1.call-update
  358.8 0.6 subtract_reduce_fusion
  359.4 20.4 %psum.46 = f32[]{:T(128)} all-reduce(f32[]{:T(128)} %subtract_reduce_fusion), channel_id=1, replica_groups=mesh['row'=4,'col'=8] {'col'}, use_global_device_ids=true, to_apply=%region_11.12 | all-reduce | flops 1 | bytes 8 | tf_op jit(solution)/shard_map/psum | solution.py:14
  379.7 6.3 %psum.47 = f32[]{:T(128)} all-reduce(f32[]{:T(128)} %psum.46), channel_id=1, replica_groups=mesh['row'=4,'col'=8] {'row'}, use_global_device_ids=true, to_apply=%region_12.13 | all-reduce | flops 1 | bytes 8 | tf_op jit(solution)/shard_map/psum | solution.py:15
  386.7 5.9 %all-reduce.7.cloned.1.call-done = (f32[128,256]{1,0:T(8,128)}, f32[256,128]{1,0:T(8,128)}) async-done(((f32[128,256]{1,0:T(8,128)}, f32[256,128]{1,0:T(8,128)}), (f32[128,256]{1,0:T(8,128)}, f32[256,128]{1,0:T(8,128)})) %all-reduce.7.cloned.1.call-update) | async-done | bytes 262160 | tf_op jit(solution)/shard_map/psum | solution.py:15
  392.5 1.6 copy.56
  394.1 1.6 copy.57
  (13 shorter events, 0.1 us)
Async XLA Ops:
  7.2 104.5 %copy-start = (bf16[256,128]{1,0:T(8,128)(2,1)S(1)}, bf16[256,128]{1,0:T(8,128)(2,1)}, u32[]{:S(2)}) copy-start(bf16[256,128]{1,0:T(8,128)(2,1)} %param.11) | copy-start | bytes 196612
  7.2 104.4 %reduce-scatter.5.cloned.1.call-start = ((), (), s32[]{:S(2)}) async-start(), calls=%async_computation.4 | async-start | bytes 1179648 | tf_op jit(solution)/shard_map/reduce_scatter | solution.py:65
  17.6 14.5 %copy-start.6 = (s32[1,128]{1,0:T(1,128)S(1)}, s32[1,128]{1,0:T(1,128)}, u32[]{:S(2)}) copy-start(s32[1,128]{1,0:T(1,128)} %param.13) | copy-start | bytes 1540
  32.0 3.6 copy-start.4
  32.0 3.7 copy-start.2
  32.0 3.7 copy-start.3
  32.1 149.0 %copy-start.5 = (s32[128]{0:T(128)S(1)}, s32[128]{0:T(128)}, u32[]{:S(2)}) copy-start(s32[128]{0:T(128)} %param.12) | copy-start | bytes 1540
  46.9 134.2 %reduce-scatter.7.cloned.1.call-start = ((), (), s32[]{:S(2)}) async-start(), calls=%async_computation.5 | async-start | bytes 589824 | tf_op jit(solution)/shard_map/reduce_scatter | solution.py:74
  111.6 150.5 %copy-start.1 = (f32[128,256]{1,0:T(8,128)S(1)}, f32[128,256]{1,0:T(8,128)}, u32[]{:S(2)}) copy-start(f32[128,256]{1,0:T(8,128)} %reduce-scatter.5.cloned.1.call-done) | copy-start | bytes 393220
  119.4 108.9 %reduce-scatter.9.cloned.1.call-start = ((), (), s32[]{:S(2)}) async-start(), calls=%async_computation.6 | async-start | bytes 327680 | tf_op jit(solution)/shard_map/reduce_scatter | solution.py:47
  210.5 73.5 %reduce-scatter.11.cloned.1.call-start = ((), (), s32[]{:S(2)}) async-start(), calls=%async_computation.7 | async-start | bytes 655360 | tf_op jit(solution)/shard_map/reduce_scatter | solution.py:47
  262.1 96.6 %all-reduce.5.cloned.1.call-start = ((), (), s32[]{:S(2)}) async-start(), calls=%async_computation.8 | async-start | bytes 524288 | tf_op jit(solution)/shard_map/psum | solution.py:14
  285.8 106.7 %all-reduce.7.cloned.1.call-start = ((), (), s32[]{:S(2)}) async-start(), calls=%async_computation.9 | async-start | bytes 524288 | tf_op jit(solution)/shard_map/psum | solution.py:15
Sparse Core Ops, SparseCore 0:
  47.0 64.5 reduce-scatter.4
  119.5 61.4 reduce-scatter.6
  210.6 17.5 reduce-scatter.8
  262.2 21.6 reduce-scatter.10
  287.9 70.8 all-reduce.4
  361.1 31.3 all-reduce.6
